TPU v7x, 32 devices: a whole 2x2x4 slice. The times are simulated.
32 devices in a mesh: slab: 4 (over y, core), sub: 8 (over z, x).
Axes of the slice: x: 2, y: 2, z: 4, core: 2. Of those that a mesh axis runs over, the one named last changes fastest.
Arguments:
- positions: float32 [3, 2097152], P(None, ('slab', 'sub')), may hold values from 0 to 32, as said below
- masses: float32 [2097152], P(('slab', 'sub')), may hold values from 0.001 to 0.01
- leaf_counts: int32 [8192], P(('slab', 'sub')), may hold values from 64 to 256, as said below
- send_leaves: int32 [32, 256], P(('slab', 'sub')), may hold values from 0 to 255, as said below
- send_parents: int32 [32, 64], P(('slab', 'sub')), may hold values from 0 to 31, as said below
- near_pairs: int32 [32, 3, 256], P(('slab', 'sub')), may hold values from -1 to 511, as said below
- far_pairs: int32 [32, 3, 1024], P(('slab', 'sub')), may hold values from -1 to 511, as said below
- parent_pairs: int32 [32, 3, 64], P(('slab', 'sub')), may hold values from -1 to 95, as said below
Outputs:
- field: float32 [4, 2097152], P(None, ('slab', 'sub'))
Inputs may be any that keep to these rules, and one draw needn't show every extreme that they name: `positions`: the coordinates of a body of leaf c on device (s, u) lie within one unit above that leaf's integer coordinates along each dimension. `leaf_counts`: every device has a leaf whose 256 slots are all used. `send_leaves`: within one direction of a row, the 64 leaves are different. `send_parents`: within one direction of a row, the 16 parent cells are different. `near_pairs`: row 0 is an own leaf, row 1 a leaf table entry or -1 for an unused entry (unused entries come last), row 2 the z image -1, 0 or 1 (0 where unused). Own pairs have a < b; no pair repeats; pairs are leaves at most one leaf apart along each dimension after the image. `far_pairs`: as near_pairs, for leaves whose squared separation after the image is 4 to 12 leaf units. `parent_pairs`: as near_pairs, for parent cells whose squared separation after the image is 2 parent units or more, with the parent table.
All inputs are finite; a program needn't handle non-finite values.
Results may differ from a plain program's by a relative error of at most 0.0003.
Values sent between devices are 32-bit elements; how exact they have to be, the bound alone decides.
No kernel may reach another device: no remote copies, remote signals or barrier semaphores. Data moves between devices by JAX's collectives and lax.ppermute only.
A program may use at most 320 MiB of HBM per device.

v0:
```python
import functools
import math

import jax
import jax.numpy as jnp
import ml_dtypes
import numpy as np
from jax import lax
from jax.experimental import pallas as pl
from jax.experimental.pallas import tpu as pltpu
from jax.sharding import PartitionSpec as P

CX = 2
CY = 4
CZ = 32

soft_square = 0.0025
slab_steps = (1, 0, 1, 1)
sub_steps = (0, 1, 1, -1)

LEAVES = CX * CY * CZ
PARENTS = LEAVES // 8
SLOTS = LEAVES // 4
PSLOTS = PARENTS // 2
HALF = 128
LEAF = 2 * HALF
BODY_ROWS = 8 * SLOTS
CELL_ROWS = SLOTS // 2
PACK_ROWS = BODY_ROWS + CELL_ROWS
GROUP = 8
bf16 = jnp.bfloat16
f32 = jnp.float32
i32 = jnp.int32

MULTI = [
    (i, j, n - i - j) for n in range(5) for i in range(n, -1, -1) for j in range(n - i, -1, -1)
]
PLACE = {alpha: at for at, alpha in enumerate(MULTI)}
TERMS = len(MULTI)
CENTRE = TERMS
LIVE = TERMS + 3
SIZES = (256, 192, 160, 128, 96)
EVERY_SIZE = tuple((size, at) for at, size in enumerate(SIZES))
SOME_SIZES = ((256, 0), (192, 2), (128, 4))
LIST = 384
STEPS_AT = LIST - 8
FEATS = 40
OWN = LEAVES + PARENTS
ENTRIES = 640
FAR_BLOCKS = 5


def fact(alpha):
    return math.prod(math.factorial(a) for a in alpha)


def added(alpha, beta):
    return tuple(a + b for a, b in zip(alpha, beta))


def taken(alpha, beta):
    return tuple(a - b for a, b in zip(alpha, beta))


def octant(at):
    return tuple(0.5 if bit else -0.5 for bit in (at >> 2 & 1, at >> 1 & 1, at & 1))


def power(delta, alpha):
    return math.prod(d**a for d, a in zip(delta, alpha))


def shift_matrices():
    up = np.zeros((8, 128, 128), np.float32)
    down = np.zeros((8, 128, 128), np.float32)
    for at in range(8):
        delta = octant(at)
        for alpha in MULTI:
            for beta in MULTI:
                rest = taken(alpha, beta)
                if min(rest) < 0:
                    continue
                choose = math.prod(math.comb(a, b) for a, b in zip(alpha, beta))
                up[at, PLACE[beta], PLACE[alpha]] = choose * power(delta, rest)
                down[at, PLACE[alpha], PLACE[beta]] = power(delta, rest) / fact(rest)
    return up.reshape(8 * 128, 128), down.transpose(1, 0, 2).reshape(128, 8 * 128)


UP, DOWN = shift_matrices()


def row_ids(shape):
    return lax.broadcasted_iota(i32, shape, 0)


def lane_ids(shape):
    return lax.broadcasted_iota(i32, shape, 1)


def monomials(x, y, z):
    table = {(0, 0, 0): None}
    axes = (x, y, z)
    for alpha in MULTI[1:]:
        lead = max(axis for axis in range(3) if alpha[axis])
        less = tuple(a - (axis == lead) for axis, a in enumerate(alpha))
        table[alpha] = axes[lead] if table[less] is None else table[less] * axes[lead]
    return table


def split3(value):
    high = value.astype(bf16).astype(f32)
    rest = value - high
    middle = rest.astype(bf16).astype(f32)
    return high, middle, rest - middle


def soft_parts():
    rest = np.float32(soft_square)
    parts = []
    for _ in range(3):
        part = np.float32(rest.astype(ml_dtypes.bfloat16))
        parts.append(float(part))
        rest = np.float32(rest - part)
    return parts


SOFT = soft_parts()


def spread(tile):
    row = row_ids((8, HALF))
    turned = pltpu.roll(tile, 4, 0)
    low = row < 4
    return jnp.concatenate([jnp.where(low, tile, turned), jnp.where(low, turned, tile)], 1)


def fold(field):
    row = row_ids((8, HALF))
    return jnp.where(row < 4, field[:, :HALF], pltpu.roll(field[:, HALF:], 4, 0))


def offset_rows(ox, oy, oz):
    row = row_ids((8, LEAF)) & 3
    return jnp.where(row == 1, ox, jnp.where(row == 2, oy, jnp.where(row == 3, oz, 0.0)))


def features(tile, offset, as_row, as_column, as_weight):
    wide = spread(tile)
    row = row_ids((8, LEAF))
    first = (row & 3) == 0
    low = row < 4
    weight = jnp.broadcast_to(wide[0:1], (8, LEAF))
    x = jnp.where(first, 0.0, wide + offset)
    square = x * x
    pairwise = square + pltpu.roll(square, 1, 0)
    q = pairwise + pltpu.roll(pairwise, 2, 0)
    y = jnp.where(first, q, x)
    zero = jnp.zeros((8, LEAF), f32)
    out = [x, q]
    if as_row or as_column or as_weight:
        h, m, l = split3(y)
    if as_row:
        part_a = jnp.where(row == 4, m, h)
        part_b = jnp.where(row == 0, l, jnp.where(row == 4, 1.0, m))
        part_c = jnp.where(first, 1.0, jnp.where(low, h, l))
        part_d = jnp.where(row < 3, 1.0, 0.0)
        out.append(jnp.concatenate([part_a, part_b, part_c, part_d], 0).astype(bf16))
    if as_column:
        scale = jnp.where(first, 1.0, -2.0)
        h2, m2, l2 = h * scale, m * scale, l * scale
        mixed = jnp.where(low, h2, m2)
        part_a = jnp.where(first, 1.0, mixed)
        part_b = jnp.where(row == 0, 1.0, jnp.where(row == 4, h, mixed))
        part_c = jnp.where(row == 0, m, jnp.where(row == 4, l, jnp.where(low, l2, h2)))
        part_d = jnp.where(
            row == 0, SOFT[0], jnp.where(row == 1, SOFT[1], jnp.where(row == 2, SOFT[2], 0.0))
        )
        out.append(jnp.concatenate([part_a, part_b, part_c, part_d], 0).astype(bf16))
    if as_weight:
        heavy = jnp.where(low, y, 1.0) * weight
        out.append(jnp.concatenate(list(split3(heavy)) + [zero], 0).astype(bf16))
    return out


def field_of(sums, x, q):
    total = sums[0:8] + sums[8:16] + sums[16:24]
    row = row_ids((8, LEAF))
    first = (row & 3) == 0
    plain = pltpu.roll(total, 4, 0)
    inner = total - jnp.where(first, q - soft_square, x) * plain
    along = x * inner
    dots = along[1:2] + along[2:3] + along[3:4]
    return fold(jnp.where(row == 0, 2.0 * dots - inner, inner))


def cubes(row_part, column_part):
    square = lax.dot_general(
        row_part, column_part, (((0,), (0,)), ((), ())), preferred_element_type=f32
    )
    inverse = lax.rsqrt(square)
    return inverse * inverse * inverse


def padded(sums):
    lanes = sums.shape[1]
    if lanes == LEAF:
        return sums
    return jnp.concatenate([sums, jnp.zeros((sums.shape[0], LEAF - lanes), f32)], 1)


def pipeline(words, at, group, plan, early, late):
    @pl.when(words[at, STEPS_AT + len(SIZES) - 1] > 0)
    def _():
        for u in range(group):
            early(SIZES[0], 0, 0, u)

    begin = jnp.int32(0)
    for size, last in plan:

        def step(k, carry, size=size):
            for slot in range(2):
                done = []
                for u in range(group):
                    done.append(late(size, 2 * k + slot, slot, u))
                    early(size, 2 * k + slot + 1, 1 - slot, u)
                for store in done:
                    store()
            return carry

        end = words[at, STEPS_AT + last]
        lax.fori_loop(begin, end, step, 0)
        begin = end


def placing(places):
    slab_count, sub_count = places
    slab_at = lax.axis_index("slab")
    sub_at = lax.axis_index("sub")
    numbers = [slab_at * CX, sub_at * CY]
    for way in range(4):
        reach_x = slab_at + slab_steps[way]
        reach_y = sub_at + sub_steps[way]
        numbers.append(jnp.where(reach_x >= slab_count, slab_count * CX, 0))
        high = jnp.where(reach_y >= sub_count, sub_count * CY, 0)
        numbers.append(jnp.where(reach_y < 0, -sub_count * CY, high))
    return numbers


def jump_of(place, way):
    jump_x = jnp.int32(0)
    jump_y = jnp.int32(0)
    for at in range(4):
        jump_x = jnp.where(way == at, place[2 + 2 * at], jump_x)
        jump_y = jnp.where(way == at, place[3 + 2 * at], jump_y)
    return jump_x.astype(f32), jump_y.astype(f32)


def leaf_centre(place, leaf):
    return (
        -(place[0] + leaf // (CY * CZ)).astype(f32) - 0.5,
        -(place[1] + leaf // CZ % CY).astype(f32) - 0.5,
        -(leaf % CZ).astype(f32) - 0.5,
    )


def tall(part):
    rows = part.shape[0]
    if rows == LEAF:
        return part
    return jnp.concatenate([part, jnp.zeros((LEAF - rows, LEAF), bf16)], 0)


def halves(c):
    high = c.astype(bf16)
    return high, (c - high.astype(f32)).astype(bf16)


def self_loop(words, at, group, plan, place, bodies, field, scratch):
    high_refs, low_refs, weight_refs, spot_refs = scratch

    def early(size, k, slot, u):
        leaf = words[at, k * group + u]
        x, q, rows, columns, weights = features(
            bodies[leaf], offset_rows(*leaf_centre(place, leaf & (LEAVES - 1))), True, True, True
        )
        wide = LEAF if size > HALF else HALF
        high, low = halves(cubes(rows[:, :size], columns[:, :wide]))
        high_refs[slot][u, :size, :wide] = high
        low_refs[slot][u, :size, :wide] = low
        weight_refs[slot][u] = weights
        spot_refs[slot][u, 0] = x
        spot_refs[slot][u, 1] = q

    def late(size, k, slot, u):
        leaf = words[at, k * group + u]
        wide = LEAF if size > HALF else HALF
        w = weight_refs[slot][u, :, :size]
        sums = jnp.dot(
            w, high_refs[slot][u, :size, :wide], preferred_element_type=f32
        ) + jnp.dot(w, low_refs[slot][u, :size, :wide], preferred_element_type=f32)
        result = field_of(padded(sums), spot_refs[slot][u, 0], spot_refs[slot][u, 1])
        itself = jnp.where((row_ids((8, HALF)) & 3) == 0, bodies[leaf], 0.0)
        result = result + itself * soft_square**-0.5

        def store():
            field[leaf] = result

        return store

    pipeline(words, at, group, plan, early, late)


def pair_loop(
    words, at, group, plan, place, jumping, bodies, others, field, other_field, scratch
):
    high_refs, low_refs, across_refs, row_refs, column_refs, spot_refs = scratch
    turned = (((1,), (1,)), ((), ()))

    def unpack(k, u):
        word = words[at, k * group + u]
        return word & 511, word >> 9 & 511, word >> 18 & 1, (word >> 19 & 3) - 1, word >> 21 & 7

    def early(size, k, slot, u):
        row_leaf, column_leaf, swapped, lift, way = unpack(k, u)
        frame = jnp.where(swapped == 1, column_leaf, row_leaf) & (LEAVES - 1)
        cx, cy, cz = leaf_centre(place, frame)
        raised = (lift * CZ).astype(f32)
        swap = (swapped == 1).astype(f32)
        jump_x, jump_y = jump_of(place, way) if jumping else (0.0, 0.0)
        row_offset = offset_rows(cx, cy, cz + swap * raised)
        column_offset = offset_rows(cx + jump_x, cy + jump_y, cz + (1.0 - swap) * raised)
        xr, qr, rows, row_weights = features(bodies[row_leaf], row_offset, True, False, True)
        xc, qc, columns, column_weights = features(
            others[column_leaf], column_offset, False, True, True
        )
        high, low = halves(cubes(rows[:, :size], columns))
        high_refs[slot][u, :size] = high
        low_refs[slot][u, :size] = low
        if size > HALF:
            across_refs[slot][u] = tall(high).T
        row_refs[slot][u] = row_weights
        column_refs[slot][u] = column_weights
        spot_refs[slot][u, 0] = xr
        spot_refs[slot][u, 1] = qr
        spot_refs[slot][u, 2] = xc
        spot_refs[slot][u, 3] = qc

    def late(size, k, slot, u):
        row_leaf, column_leaf, _, _, _ = unpack(k, u)
        wr = row_refs[slot][u, :, :size]
        wc = column_refs[slot][u]
        high = high_refs[slot][u, :size]
        low = low_refs[slot][u, :size]
        column_sums = jnp.dot(wr, high, preferred_element_type=f32) + jnp.dot(
            wr, low, preferred_element_type=f32
        )
        row_sums = lax.dot_general(wc, low, turned, preferred_element_type=f32)
        if size > HALF:
            row_sums = padded(row_sums) + jnp.dot(
                wc, across_refs[slot][u], preferred_element_type=f32
            )
        else:
            row_sums += lax.dot_general(wc, high, turned, preferred_element_type=f32)
        row_field = field_of(padded(row_sums), spot_refs[slot][u, 0], spot_refs[slot][u, 1])
        column_field = field_of(column_sums, spot_refs[slot][u, 2], spot_refs[slot][u, 3])

        def store():
            field[row_leaf] = field[row_leaf] + row_field
            other_field[column_leaf] = other_field[column_leaf] + column_field

        return store

    pipeline(words, at, group, plan, early, late)


def pair_scratch(group):
    return (
        [pltpu.VMEM((group, LEAF, LEAF), bf16)] * 6
        + [pltpu.VMEM((group, 32, LEAF), bf16)] * 4
        + [pltpu.VMEM((group, 4, 8, LEAF), f32)] * 2
    )


def paired(scratch):
    return [scratch[at : at + 2] for at in range(0, len(scratch), 2)]


def front_kernel(places, *refs):
    stored, made, held, sems, chosen = refs[:7], refs[7:15], refs[15:23], refs[23], refs[24]
    bodies, moments, parents, words = made[:4]
    outs = made[4:]
    sources = (stored[0], stored[1], stored[2], *stored[2:])
    copies = [
        pltpu.make_async_copy(source, target, sems.at[at])
        for at, (source, target) in enumerate(zip(sources, held))
    ]
    for copy in copies:
        copy.start()
    send, send_p, counts, count_row, pairs, spots, masses, up = held
    place = placing(places)
    copies[3].wait()
    copies[4].wait()
    words[...] = work_lists(count_row[...], pairs[0], pairs[1], pairs[2])
    copies[2].wait()
    copies[5].wait()
    copies[6].wait()
    row = row_ids((8, HALF))

    def tile(g):
        count = jnp.zeros((8, HALF), i32)
        for u in range(8):
            leaf = 8 * g + u
            start = pl.multiple_of(leaf * LEAF, LEAF)
            low = spots[:, pl.ds(start, HALF)]
            high = spots[:, pl.ds(start + HALF, HALF)]
            blank = jnp.zeros((1, HALF), f32)
            bodies[pl.ds(pl.multiple_of(8 * leaf, 8), 8), :] = jnp.concatenate(
                [blank, low, blank, high], 0
            )
            count = jnp.where(row == u, counts[0, leaf], count)
        lane = lane_ids((8, HALF))
        for half in range(2):
            mass = masses[pl.ds(16 * g + half, 8, stride=2), :]
            bodies[pl.ds(64 * g + 4 * half, 8, stride=8), :] = jnp.where(
                lane + half * HALF < count, mass, 0.0
            )

    def cell_moments(g, parts):
        w, px, py, pz = parts
        cx, cy, cz = group_centre(place, g)
        axes = (px - cx, py - cy, pz - cz)
        table = {(0, 0, 0): w}
        lane = lane_ids((8, 128))
        built = jnp.zeros((8, 128), f32)
        for alpha in MULTI:
            if alpha not in table:
                lead = max(axis for axis in range(3) if alpha[axis])
                less = tuple(a - (axis == lead) for axis, a in enumerate(alpha))
                table[alpha] = table[less] * axes[lead]
            value = table[alpha]
            total = jnp.sum(value[:, :HALF] + value[:, HALF:], axis=1, keepdims=True)
            built = jnp.where(lane == PLACE[alpha], total, built)
        built = jnp.where(lane == CENTRE, cx, built)
        built = jnp.where(lane == CENTRE + 1, cy, built)
        built = jnp.where(lane == CENTRE + 2, cz, built)
        moments[pl.ds(pl.multiple_of(8 * g, 8), 8), :] = built

    batch = 4
    for u in range(batch):
        tile(u)

    def group_step(k, carry):
        groups = [batch * k + u for u in range(batch)]
        parts = [wide_rows(bodies, g) for g in groups]
        following = jnp.minimum(batch * (k + 1), LEAVES // 8 - batch)
        for u in range(batch):
            tile(following + u)
        for g, part in zip(groups, parts):
            cell_moments(g, part)
        return carry

    lax.fori_loop(0, LEAVES // 8 // batch, group_step, 0)
    kind = row & 3
    bx = place[0].astype(f32) + 0.5
    by = place[1].astype(f32) + 0.5
    bodies[8 * LEAVES : 8 * LEAVES + 8, :] = jnp.where(
        kind == 1, bx, jnp.where(kind == 2, by, jnp.where(kind == 3, 0.5, 0.0))
    )
    copies[7].wait()
    half_z = CZ // 2
    summed = jnp.zeros((PARENTS, 128), f32)
    for at in range(8):
        first = (at >> 2 & 1) * CY * CZ + (at >> 1 & 1) * CZ + (at & 1)
        piece = jnp.concatenate(
            [moments[pl.ds(first + 2 * CZ * py, half_z, stride=2), :] for py in range(CY // 2)], 0
        )
        summed = summed + jnp.dot(
            piece,
            up[128 * at : 128 * at + 128, :],
            precision=lax.Precision.HIGHEST,
            preferred_element_type=f32,
        )
    lane = lane_ids((PARENTS, 128))
    cell = row_ids((PARENTS, 128))
    summed = jnp.where(lane == CENTRE, place[0].astype(f32) + 1.0, summed)
    summed = jnp.where(
        lane == CENTRE + 1,
        place[1].astype(f32) + 1.0 + 2.0 * (cell // half_z).astype(f32),
        summed,
    )
    summed = jnp.where(lane == CENTRE + 2, 1.0 + 2.0 * (cell % half_z).astype(f32), summed)
    parents[...] = summed
    copies[0].wait()
    copies[1].wait()
    for way in range(4):

        def leaf_step(k, carry, way=way):
            leaf = send[0, way * SLOTS + k]
            outs[way][pl.ds(pl.multiple_of(8 * k, 8), 8), :] = bodies[
                pl.ds(pl.multiple_of(8 * leaf, 8), 8), :
            ]
            chosen[pl.ds(way * (SLOTS + PSLOTS) + k, 1), :] = moments[pl.ds(leaf, 1), :]
            return carry

        lax.fori_loop(0, SLOTS, leaf_step, 0, unroll=8)
        for k in range(PSLOTS):
            cell = send_p[0, way * PSLOTS + k]
            chosen[pl.ds(way * (SLOTS + PSLOTS) + SLOTS + k, 1), :] = parents[pl.ds(cell, 1), :]
        first = way * (SLOTS + PSLOTS)
        outs[way][BODY_ROWS:, :] = three_to_a_row(
            chosen[first : first + SLOTS, :], chosen[first + SLOTS : first + SLOTS + PSLOTS, :]
        )


def three_to_a_row(leaves, parents):
    rest = jnp.zeros((CELL_ROWS - parents.shape[0], 128), f32)
    return (
        leaves[:CELL_ROWS]
        + pltpu.roll(leaves[CELL_ROWS:], FEATS, 1)
        + pltpu.roll(jnp.concatenate([parents, rest], 0), 2 * FEATS, 1)
    )


def one_to_a_row(rows):
    keep = lane_ids(rows.shape) < FEATS
    parts = [rows, pltpu.roll(rows, 128 - FEATS, 1), pltpu.roll(rows, 128 - 2 * FEATS, 1)]
    parts = [jnp.where(keep, part, 0.0) for part in parts]
    return jnp.concatenate(parts[:2], 0), parts[2][:PSLOTS]


def wide_rows(bodies, g):
    return [
        jnp.concatenate(
            [bodies[pl.ds(64 * g + 4 * half + at, 8, stride=8), :] for half in range(2)], 1
        )
        for at in range(4)
    ]


def group_centre(place, g):
    cx = (place[0] + g // (CY * CZ // 8)).astype(f32) + 0.5
    cy = (place[1] + g // (CZ // 8) % CY).astype(f32) + 0.5
    base_z = (8 * (g % (CZ // 8))).astype(f32) + 0.5
    return cx, cy, row_ids((8, 1)).astype(f32) + base_z


def work_lists(counts, owned, partner, image):
    wide = (LEAVES, LEAVES)
    every = jnp.broadcast_to(counts.astype(f32), (8, LEAVES)).astype(bf16)

    def count_of(index):
        hot = jnp.where(row_ids(wide) == index, 1.0, 0.0).astype(bf16)
        return jnp.dot(every, hot, preferred_element_type=f32)[:1].astype(i32)

    mine = jnp.logical_and(partner >= 0, partner < LEAVES)
    other = partner >= LEAVES
    count_a = count_of(owned)
    count_b = count_of(partner)
    swapped = count_b < count_a
    lift = (image + 1) << 19
    own_word = (
        jnp.where(swapped, partner, owned)
        | jnp.where(swapped, owned, partner) << 9
        | jnp.where(swapped, 1, 0) << 18
        | lift
        | 4 << 21
    )
    spot = jnp.maximum(partner - LEAVES, 0)
    other_word = owned | spot << 9 | lift | (spot // SLOTS) << 21
    own_empty = LEAVES << 9 | 1 << 19 | 4 << 21
    other_empty = (4 * SLOTS) << 9 | 1 << 19 | 4 << 21
    yes = jnp.ones((1, LEAVES), jnp.bool_)
    lists = [
        (own_word, mine, jnp.minimum(count_a, count_b), own_empty, 2 * GROUP),
        (other_word, other, count_a, other_empty, GROUP),
        (lane_ids((1, LEAVES)), yes, counts, LEAVES, 2 * GROUP),
    ]
    flags = []
    for _, member, need, _, _ in lists:
        for at, size in enumerate(SIZES):
            fits = need <= size
            if at + 1 < len(SIZES):
                fits = jnp.logical_and(fits, need > SIZES[at + 1])
            flags.append(jnp.where(jnp.logical_and(member, fits), 1.0, 0.0))
    flags = jnp.concatenate(flags + [jnp.zeros((16 - len(flags), LEAVES), f32)], 0)
    before = jnp.where(row_ids(wide) < lane_ids(wide), 1.0, 0.0).astype(bf16)
    order = jnp.dot(flags.astype(bf16), before, preferred_element_type=f32)
    number = jnp.sum(flags, axis=1, keepdims=True)
    lane = lane_ids((1, LIST))
    rows = []
    for at, (word, member, _, empty, unit) in enumerate(lists):
        spot = jnp.zeros((1, LEAVES), f32)
        total = jnp.zeros((1, 1), f32)
        ends = []
        for row in range(len(SIZES) * at, len(SIZES) * (at + 1)):
            spot = spot + flags[row : row + 1] * (order[row : row + 1] + total)
            total = total + number[row : row + 1]
            ends.append((total.astype(i32) + (unit - 1)) // unit)
        spot = jnp.where(member, spot, -1.0).astype(i32)
        pieces = jnp.concatenate(
            [word & 255, word >> 8 & 255, word >> 16, jnp.zeros((5, LEAVES), i32)], 0
        )
        hot = jnp.where(row_ids(wide) == spot, 1.0, 0.0).astype(bf16)
        found = lax.dot_general(
            pieces.astype(f32).astype(bf16),
            hot,
            (((1,), (1,)), ((), ())),
            preferred_element_type=f32,
        ).astype(i32)
        joined = found[0:1] | found[1:2] << 8 | found[2:3] << 16
        joined = jnp.concatenate([joined, jnp.zeros((1, LIST - LEAVES), i32)], 1)
        joined = jnp.where(lane < total.astype(i32), joined, empty)
        for size_at, end in enumerate(ends):
            joined = jnp.where(lane == STEPS_AT + size_at, end, joined)
        rows.append(joined)
    return jnp.concatenate(rows + [jnp.zeros((5, LIST), i32)], 0)


def self_kernel(places, words, bodies, field, *scratch):
    place = placing(places)
    field[LEAVES] = jnp.zeros((8, HALF), f32)
    self_loop(words, 2, GROUP, EVERY_SIZE, place, bodies, field, paired(scratch))


def near_kernel(places, words, bodies, field_in, field, *scratch):
    place = placing(places)
    refs = paired(scratch)
    pair_loop(words, 0, GROUP, EVERY_SIZE, place, False, bodies, bodies, field, field, refs)


def derivatives(x, y, z):
    inverse = lax.rsqrt(x * x + y * y + z * z)
    square = inverse * inverse
    odd = [inverse]
    for _ in range(4):
        odd.append(odd[-1] * square)
    powers = monomials(x, y, z)
    result = {}
    for alpha in MULTI:
        degree = sum(alpha)
        total = None
        for p in range(alpha[0] // 2 + 1):
            for q in range(alpha[1] // 2 + 1):
                for s in range(alpha[2] // 2 + 1):
                    m = p + q + s
                    ways = math.prod(
                        math.factorial(a) // (2**c * math.factorial(c) * math.factorial(a - 2 * c))
                        for a, c in zip(alpha, (p, q, s))
                    )
                    sign = (-1.0) ** (degree - m)
                    double = math.prod(range(1, 2 * (degree - m), 2))
                    term = odd[degree - m] * (sign * double * ways)
                    rest = (alpha[0] - 2 * p, alpha[1] - 2 * q, alpha[2] - 2 * s)
                    if powers[rest] is not None:
                        term = term * powers[rest]
                    total = term if total is None else total + term
        result[alpha] = total
    return result


def remote_kernel(
    places,
    words,
    far,
    cells,
    bodies,
    moments,
    parents,
    in_0,
    in_1,
    in_2,
    in_3,
    field_in,
    field,
    leaf_terms,
    parent_terms,
    out_0,
    out_1,
    out_2,
    out_3,
    far_bodies,
    far_field,
    gather_a,
    gather_b,
    *scratch,
):
    place = placing(places)
    incoming = (in_0, in_1, in_2, in_3)
    outgoing = (out_0, out_1, out_2, out_3)
    for way in range(4):
        far_bodies[way * SLOTS : (way + 1) * SLOTS] = incoming[way][:BODY_ROWS, :].reshape(
            SLOTS, 8, HALF
        )
    far_bodies[4 * SLOTS] = bodies[LEAVES]
    far_field[...] = jnp.zeros_like(far_field)
    refs = paired(scratch)
    pair_loop(
        words, 1, GROUP // 2, SOME_SIZES, place, True, bodies, far_bodies, field, far_field, refs
    )
    for way in range(4):
        outgoing[way][:BODY_ROWS, :] = far_field[way * SLOTS : (way + 1) * SLOTS].reshape(
            BODY_ROWS, HALF
        )

    def moved(rows, way):
        lane = lane_ids(rows.shape)
        rows = jnp.where(lane == CENTRE, rows + place[2 + 2 * way].astype(f32), rows)
        return jnp.where(lane == CENTRE + 1, rows + place[3 + 2 * way].astype(f32), rows)

    arrived = [one_to_a_row(incoming[way][BODY_ROWS:, :]) for way in range(4)]
    table = [moments[...], parents[...]]
    for way in range(4):
        table.append(moved(arrived[way][0], way))
    for way in range(4):
        table.append(moved(arrived[way][1], way))
    table.append(jnp.zeros((ENTRIES - OWN - 4 * SLOTS - 4 * PSLOTS, 128), f32))
    columns = jnp.concatenate(table, 0).T[:FEATS]
    columns = jnp.concatenate(split3(columns), 0).astype(bf16)

    def one_hot(index, entries):
        return jnp.where(row_ids((entries, index.shape[1])) == index, 1.0, 0.0).astype(bf16)

    def joined(parts):
        return parts[:FEATS] + parts[FEATS : 2 * FEATS] + parts[2 * FEATS :]

    def far_block(block):
        if block < FAR_BLOCKS - 1:
            lanes = slice(LEAF * block, LEAF * block + LEAF)
            a, b, z = far[0, :, lanes], far[1, :, lanes], far[2, :, lanes]
            used = b >= 0
            b = jnp.where(b >= LEAVES, b + PARENTS, b)
        else:
            blank = jnp.zeros((1, 128 - cells.shape[2]), i32)
            a = jnp.concatenate([cells[0] + LEAVES, blank], 1)
            b = jnp.concatenate([cells[1], blank - 1], 1)
            z = jnp.concatenate([cells[2], blank], 1)
            used = b >= 0
            b = jnp.where(b >= PARENTS, b + (OWN + 4 * SLOTS - PARENTS), b + LEAVES)
            b = jnp.where(used, b, -1)
        a = jnp.where(used, a, -1)
        return a, b, (z * CZ).astype(f32), jnp.where(used, 1.0, 0.0)

    def far_rows(block):
        parts = range(2 * block, 2 * block + (2 if block < FAR_BLOCKS - 1 else 1))
        return [slice(FEATS * part, FEATS * part + FEATS) for part in parts]

    gather_a[...] = jnp.zeros_like(gather_a)
    gather_b[...] = jnp.zeros_like(gather_b)
    for block in range(FAR_BLOCKS):
        a, b, lift, used = far_block(block)
        place_of = row_ids((FEATS, a.shape[1]))
        got_a = joined(jnp.dot(columns[:, :OWN], one_hot(a, OWN), preferred_element_type=f32))
        got_b = joined(jnp.dot(columns, one_hot(b, ENTRIES), preferred_element_type=f32))
        got_a = jnp.where(place_of == LIVE, used, got_a)
        got_b = got_b + jnp.where(place_of == CENTRE + 2, lift, 0.0)
        for part, rows in enumerate(far_rows(block)):
            gather_a[rows, :] = got_a[:, 128 * part : 128 * part + 128]
            gather_b[rows, :] = got_b[:, 128 * part : 128 * part + 128]
    for chunk in range(2):
        start = 8 * chunk * FEATS

        def feature(ref, at, start=start):
            return ref[pl.ds(start + at, 8, stride=FEATS), :]

        def gap(axis):
            return feature(gather_a, CENTRE + axis) - feature(gather_b, CENTRE + axis)

        live = feature(gather_a, LIVE) > 0.0
        x = jnp.where(live, gap(0), 3.0)
        y = jnp.where(live, gap(1), 3.0)
        z = jnp.where(live, gap(2), 3.0)
        tensors = derivatives(x, y, z)
        held_a = {}
        held_b = {}
        for alpha in MULTI:
            held_a[alpha] = feature(gather_a, PLACE[alpha]) * (-1.0 / fact(alpha))
            held_b[alpha] = feature(gather_b, PLACE[alpha]) * (
                -((-1.0) ** sum(alpha)) / fact(alpha)
            )
        for beta in MULTI:
            to_a = None
            to_b = None
            for alpha in MULTI:
                if sum(alpha) + sum(beta) > 4:
                    continue
                tensor = tensors[added(alpha, beta)]
                term_a = held_b[alpha] * tensor
                term_b = held_a[alpha] * tensor
                to_a = term_a if to_a is None else to_a + term_a
                to_b = term_b if to_b is None else to_b + term_b
            if sum(beta) % 2:
                to_b = -to_b
            gather_a[pl.ds(start + PLACE[beta], 8, stride=FEATS), :] = to_a
            gather_b[pl.ds(start + PLACE[beta], 8, stride=FEATS), :] = to_b
    sums_a = jnp.zeros((3 * FEATS, OWN), f32)
    sums_b = jnp.zeros((3 * FEATS, ENTRIES), f32)
    turned = (((1,), (1,)), ((), ()))
    for block in range(FAR_BLOCKS):
        a, b, _, _ = far_block(block)
        rows = far_rows(block)
        got_a = jnp.concatenate([gather_a[part, :] for part in rows], 1)
        got_b = jnp.concatenate([gather_b[part, :] for part in rows], 1)
        parts_a = jnp.concatenate(split3(got_a), 0).astype(bf16)
        parts_b = jnp.concatenate(split3(got_b), 0).astype(bf16)
        hot_a = one_hot(a, OWN)
        hot_b = one_hot(b, ENTRIES)
        sums_a = sums_a + lax.dot_general(parts_a, hot_a, turned, preferred_element_type=f32)
        sums_b = sums_b + lax.dot_general(parts_b, hot_b, turned, preferred_element_type=f32)
    got_a = jnp.concatenate([joined(sums_a), jnp.zeros((128 - FEATS, OWN), f32)], 0)
    got_b = jnp.concatenate([joined(sums_b), jnp.zeros((128 - FEATS, ENTRIES), f32)], 0)
    keep = lane_ids((1, 128)) < TERMS
    terms_a = jnp.where(keep, got_a.T, 0.0)
    terms_b = jnp.where(keep, got_b.T, 0.0)
    leaf_terms[...] = terms_a[:LEAVES] + terms_b[:LEAVES]
    parent_terms[...] = terms_a[LEAVES:OWN] + terms_b[LEAVES:OWN]
    leaf_start = OWN
    parent_start = OWN + 4 * SLOTS
    for way in range(4):
        leaf_first = leaf_start + way * SLOTS
        parent_first = parent_start + way * PSLOTS
        outgoing[way][BODY_ROWS:, :] = three_to_a_row(
            terms_b[leaf_first : leaf_first + SLOTS],
            terms_b[parent_first : parent_first + PSLOTS],
        )


def back_kernel(
    places,
    counts,
    send,
    send_p,
    bodies,
    field_in,
    leaf_in,
    parent_in,
    down,
    in_0,
    in_1,
    in_2,
    in_3,
    result,
    field,
    leaf_terms,
    parent_terms,
    tiles,
    arrived,
    out,
    sems,
):
    place = placing(places)
    incoming = (in_0, in_1, in_2, in_3)
    leaf_terms[...] = leaf_in[...]
    parent_terms[...] = parent_in[...]
    for way in range(4):
        leaf_rows, parent_rows = one_to_a_row(incoming[way][BODY_ROWS:, :])
        arrived[:SLOTS, :] = leaf_rows
        arrived[SLOTS:, :] = parent_rows

        def leaf_step(g, carry, way=way):
            at = [16 * g + u for u in range(16)]
            leaves = [send[0, way * SLOTS + k] for k in at]
            bodies_now = [
                field[leaf] + incoming[way][pl.ds(pl.multiple_of(8 * k, 8), 8), :]
                for k, leaf in zip(at, leaves)
            ]
            terms_now = [
                leaf_terms[pl.ds(leaf, 1), :] + arrived[pl.ds(k, 1), :]
                for k, leaf in zip(at, leaves)
            ]
            for leaf, value, terms in zip(leaves, bodies_now, terms_now):
                field[leaf] = value
                leaf_terms[pl.ds(leaf, 1), :] = terms
            return carry

        lax.fori_loop(0, SLOTS // 16, leaf_step, 0)
        chosen = [send_p[0, way * PSLOTS + k] for k in range(PSLOTS)]
        terms_now = [
            parent_terms[pl.ds(cell, 1), :] + arrived[pl.ds(SLOTS + k, 1), :]
            for k, cell in enumerate(chosen)
        ]
        for cell, terms in zip(chosen, terms_now):
            parent_terms[pl.ds(cell, 1), :] = terms
    half_z = CZ // 2
    for at in range(8):
        moved = jnp.dot(
            parent_terms[...],
            down[:, 128 * at : 128 * at + 128],
            precision=lax.Precision.HIGHEST,
            preferred_element_type=f32,
        )
        first = (at >> 2 & 1) * CY * CZ + (at >> 1 & 1) * CZ + (at & 1)
        for py in range(CY // 2):
            rows = pl.ds(first + 2 * CZ * py, half_z, stride=2)
            leaf_terms[rows, :] = leaf_terms[rows, :] + moved[half_z * py : half_z * py + half_z]

    lane = lane_ids((8, 128))
    inverse_factorials = jnp.zeros((8, 128), f32)
    for alpha in MULTI:
        inverse_factorials = jnp.where(lane == PLACE[alpha], 1.0 / fact(alpha), inverse_factorials)

    def group_step(g, carry):
        rows = pl.ds(pl.multiple_of(8 * g, 8), 8)
        cx, cy, cz = group_centre(place, g)
        _, px, py, pz = wide_rows(bodies, g)
        x, y, z = px - cx, py - cy, pz - cz
        terms = leaf_terms[rows, :] * inverse_factorials

        def coefficient(*alpha):
            at = PLACE[alpha]
            return jnp.broadcast_to(terms[:, at : at + 1], (8, LEAF))

        def nested(values, t):
            total, slope = values[-1], None
            for value in values[-2::-1]:
                slope = total if slope is None else slope * t + total
                total = total * t + value
            return total, slope

        def plain(values, t):
            total = values[-1]
            for value in values[-2::-1]:
                total = total * t + value
            return total

        by_x = []
        by_x_y = []
        by_x_z = []
        for i in range(5):
            in_z = [
                nested([coefficient(i, j, k) for k in range(5 - i - j)], z) for j in range(5 - i)
            ]
            value, slope = nested([pair[0] for pair in in_z], y)
            by_x.append(value)
            if i < 4:
                by_x_y.append(slope)
                by_x_z.append(plain([pair[1] for pair in in_z[:-1]], y))
        value, slope = nested(by_x, x)
        values = [value, -slope, -plain(by_x_y, x), -plain(by_x_z, x)]
        for at, value in enumerate(values):
            tiles[pl.ds(64 * g + at, 8, stride=8), :] = value[:, :HALF]
            tiles[pl.ds(64 * g + 4 + at, 8, stride=8), :] = value[:, HALF:]
        row = row_ids((8, HALF))
        body = lane_ids((8, HALF)) + jnp.where(row < 4, 0, HALF)
        for u in range(8):
            leaf = 8 * g + u
            tile = tiles[pl.ds(pl.multiple_of(8 * leaf, 8), 8), :] + field[leaf]
            tile = jnp.where(body < counts[leaf], tile, 0.0)
            start = pl.multiple_of(leaf * LEAF, LEAF)
            out[:, pl.ds(start, HALF)] = tile[:4]
            out[:, pl.ds(start + HALF, HALF)] = tile[4:]
        return carry

    copies = []
    for part in range(4):
        groups = LEAVES // 32
        lax.fori_loop(groups * part, groups * (part + 1), group_step, 0, unroll=4)
        lanes = pl.ds(8 * LEAF * groups * part, 8 * LEAF * groups)
        copies.append(
            pltpu.make_async_copy(out.at[:, lanes], result.at[:, lanes], sems.at[part])
        )
        copies[-1].start()
    for copy in copies:
        copy.wait()


VMEM = pl.BlockSpec(memory_space=pltpu.VMEM)
SMEM = pl.BlockSpec(memory_space=pltpu.SMEM)
HBM = pl.BlockSpec(memory_space=pltpu.HBM)
params = pltpu.CompilerParams(vmem_limit_bytes=20 * 1024 * 1024)
packed = jax.ShapeDtypeStruct((PACK_ROWS, 128), f32)
tiled = jax.ShapeDtypeStruct((LEAVES + 1, 8, HALF), f32)
heavy = pl.CostEstimate(flops=20_000_000_000, bytes_accessed=2_000_000, transcendentals=0)


def shaped(*dims):
    return jax.ShapeDtypeStruct(dims, f32)


def on_device(
    positions, masses, leaf_counts, send_leaves, send_parents, near_pairs, far_pairs, parent_pairs
):
    slab_count = lax.axis_size("slab")
    sub_count = lax.axis_size("sub")
    places = (slab_count, sub_count)

    def rows_first(lists):
        return jnp.transpose(lists, (1, 0, 2))

    sent = pl.pallas_call(
        functools.partial(front_kernel, places),
        out_shape=[shaped(8 * LEAVES + 8, HALF), shaped(LEAVES, 128), shaped(PARENTS, 128)]
        + [jax.ShapeDtypeStruct((8, LIST), i32)]
        + [packed] * 4,
        in_specs=[HBM] * 7,
        out_specs=[VMEM] * 8,
        scratch_shapes=[
            pltpu.SMEM(send_leaves.shape, i32),
            pltpu.SMEM(send_parents.shape, i32),
            pltpu.SMEM((1, LEAVES), i32),
            pltpu.VMEM((1, LEAVES), i32),
            pltpu.VMEM((3, 1, near_pairs.shape[2]), i32),
            pltpu.VMEM(positions.shape, f32),
            pltpu.VMEM((2 * LEAVES, HALF), f32),
            pltpu.VMEM(UP.shape, f32),
            pltpu.SemaphoreType.DMA((8,)),
            pltpu.VMEM((4 * (SLOTS + PSLOTS), 128), f32),
        ],
        compiler_params=params,
        name="moments_and_packing",
    )(
        *(
            pltpu.with_memory_space_constraint(value, pltpu.HBM)
            for value in (
                send_leaves,
                send_parents,
                leaf_counts.reshape(1, LEAVES),
                rows_first(near_pairs),
                positions,
                masses.reshape(2 * LEAVES, HALF),
                jnp.asarray(UP),
            )
        )
    )
    bodies = sent[0].reshape(LEAVES + 1, 8, HALF)
    moments, parents, words = sent[1:4]

    def exchange(value, way, back):
        pairs = []
        for s in range(slab_count):
            for u in range(sub_count):
                here = s * sub_count + u
                there = (s + slab_steps[way]) % slab_count * sub_count + (
                    u + sub_steps[way]
                ) % sub_count
                pairs.append((here, there) if back else (there, here))
        return lax.ppermute(value, ("slab", "sub"), pairs)

    incoming = [exchange(sent[4 + way], way, False) for way in range(4)]

    field = pl.pallas_call(
        functools.partial(self_kernel, places),
        out_shape=tiled,
        in_specs=[SMEM, VMEM],
        out_specs=VMEM,
        scratch_shapes=[pltpu.VMEM((GROUP, LEAF, LEAF), bf16)] * 4
        + [pltpu.VMEM((GROUP, 32, LEAF), bf16)] * 2
        + [pltpu.VMEM((GROUP, 2, 8, LEAF), f32)] * 2,
        compiler_params=params,
        cost_estimate=heavy,
        name="self_pairs",
    )(words, bodies)

    middle = pl.pallas_call(
        functools.partial(remote_kernel, places),
        out_shape=[tiled, shaped(LEAVES, 128), shaped(PARENTS, 128)] + [packed] * 4,
        in_specs=[SMEM] + [VMEM] * 10,
        out_specs=[VMEM] * 7,
        scratch_shapes=[
            pltpu.VMEM((4 * SLOTS + 1, 8, HALF), f32),
            pltpu.VMEM((4 * SLOTS + 1, 8, HALF), f32),
            pltpu.VMEM((16 * FEATS, 128), f32),
            pltpu.VMEM((16 * FEATS, 128), f32),
        ]
        + pair_scratch(GROUP // 2),
        compiler_params=params,
        input_output_aliases={10: 0},
        name="pairs_with_others",
    )(
        words,
        rows_first(far_pairs),
        rows_first(parent_pairs),
        bodies,
        moments,
        parents,
        *incoming,
        field,
    )
    field, leaf_terms, parent_terms = middle[:3]
    arrived = [exchange(middle[3 + way], way, True) for way in range(4)]

    field = pl.pallas_call(
        functools.partial(near_kernel, places),
        out_shape=tiled,
        in_specs=[SMEM] + [VMEM] * 2,
        out_specs=VMEM,
        scratch_shapes=pair_scratch(GROUP),
        compiler_params=params,
        cost_estimate=heavy,
        input_output_aliases={2: 0},
        name="own_pairs",
    )(words, bodies, field)

    return pl.pallas_call(
        functools.partial(back_kernel, places),
        out_shape=[shaped(4, LEAVES * LEAF), tiled],
        in_specs=[SMEM] * 3 + [VMEM] * 9,
        out_specs=[HBM, VMEM],
        input_output_aliases={4: 1},
        scratch_shapes=[
            pltpu.VMEM((LEAVES, 128), f32),
            pltpu.VMEM((PARENTS, 128), f32),
            pltpu.VMEM((8 * LEAVES, HALF), f32),
            pltpu.VMEM((SLOTS + PSLOTS, 128), f32),
            pltpu.VMEM((4, LEAVES * LEAF), f32),
            pltpu.SemaphoreType.DMA((4,)),
        ],
        compiler_params=params,
        name="shift_and_evaluate",
    )(
        leaf_counts,
        send_leaves,
        send_parents,
        sent[0],
        field,
        leaf_terms,
        parent_terms,
        jnp.asarray(DOWN),
        *arrived,
    )[0]


def solution(mesh):
    return jax.shard_map(
        on_device,
        mesh=mesh,
        in_specs=(
            P(None, ("slab", "sub")),
            P(("slab", "sub")),
            P(("slab", "sub")),
            P(("slab", "sub"), None),
            P(("slab", "sub"), None),
            P(("slab", "sub"), None, None),
            P(("slab", "sub"), None, None),
            P(("slab", "sub"), None, None),
        ),
        out_specs=P(None, ("slab", "sub")),
        check_vma=False,
    )
```

profile of v0, /device:TPU:1, one launch (start us, length us, event | category | flops | bytes accessed | tf_op | source)
XLA Modules:
  0.0 73.8 jit_solution(7923922126975963781)
XLA Ops:
  0.0 6.1 %moments_and_packing.1 = (f32[2056,128]{1,0:T(8,128)S(1)}, f32[256,128]{1,0:T(8,128)S(1)}, f32[32,128]{1,0:T(8,128)S(1)}, s32[8,384]{1,0:T(8,128)S(1)}, f32[544,...) custom-call(s32[1,256]{1,0:T(1,128)} %send.1, s32[1,64]{1,0:T(1,128)} %send_p.1, ...), custom_call_target="tpu_custom_call" | custom-call | tf_op jit(solution)/shard_map/moments_and_packing/pallas_call | solution.py:989
  6.2 0.1 collective-permute-start
  6.3 5.7 %collective-permute-start.1 = (f32[544,128]{1,0:T(8,128)S(1)}, f32[544,128]{1,0:T(8,128)S(1)}, u32[]{:S(2)}, u32[]{:S(2)}) collective-permute-start(f32[544,128]{1,0:T(8,128)S(1)} %get-tuple-element.26), channel_id=1, source_target_pairs={{1,0},{2,1},{3,2},{4,3},{5,4},{6,5},{7,6},{0,7},{9,8},{10,9},{11,1... | collective-permute-start | bytes 835592 | tf_op jit(solution)/shard_map/ppermute | solution.py:1036
  12.0 1.4 %collective-permute-start.2 = (f32[544,128]{1,0:T(8,128)S(1)}, f32[544,128]{1,0:T(8,128)S(1)}, u32[]{:S(2)}, u32[]{:S(2)}) collective-permute-start(f32[544,128]{1,0:T(8,128)S(1)} %get-tuple-element.27), channel_id=1, source_target_pairs={{9,0},{10,1},{11,2},{12,3},{13,4},{14,5},{15,6},{8,7},{17,8},{18,9... | collective-permute-start | bytes 835592 | tf_op jit(solution)/shard_map/ppermute | solution.py:1036
  13.3 1.3 %collective-permute-start.3 = (f32[544,128]{1,0:T(8,128)S(1)}, f32[544,128]{1,0:T(8,128)S(1)}, u32[]{:S(2)}, u32[]{:S(2)}) collective-permute-start(f32[544,128]{1,0:T(8,128)S(1)} %get-tuple-element.28), channel_id=1, source_target_pairs={{15,0},{8,1},{9,2},{10,3},{11,4},{12,5},{13,6},{14,7},{23,8},{16,9... | collective-permute-start | bytes 835592 | tf_op jit(solution)/shard_map/ppermute | solution.py:1036
  14.7 18.5 %self_pairs.1.field_in = f32[257,8,128]{2,1,0:T(8,128)S(1)} custom-call(s32[8,384]{1,0:T(8,128)S(1)} %get-tuple-element.22.words, f32[257,8,128]{2,1,0:T(8,128)S(1)} %bitcast.6), custom_call_target="tpu_custom_call" | custom-call | flops 20000000000 | bytes 2000000 | tf_op jit(solution)/shard_map/self_pairs/pallas_call | solution.py:1040
  33.1 0.0 collective-permute-done.in_0
  33.1 0.0 collective-permute-done.1.in_1
  33.2 0.0 collective-permute-done.2.in_2
  33.2 0.0 collective-permute-done.3.in_3
  33.2 0.0 copy-done.1
  33.2 0.0 copy-done.5
  33.2 10.7 %pairs_with_others.1 = (f32[257,8,128]{2,1,0:T(8,128)S(1)}, f32[256,128]{1,0:T(8,128)S(1)}, f32[32,128]{1,0:T(8,128)S(1)}, f32[544,128]{1,0:T(8,128)S(1)}, f32[5...) custom-call(s32[8,384]{1,0:T(8,128)S(1)} %get-tuple-element.22.words, ...), custom_call_target="tpu_custom_call", output_to_operand_aliasing={{0}: (10, {})} | custom-call | tf_op jit(solution)/shard_map/pairs_with_others/pallas_call | solution.py:1053
  43.9 0.1 collective-permute-start.4
  44.0 0.1 collective-permute-start.5
  44.0 0.1 collective-permute-start.6
  44.1 3.5 %collective-permute-start.7 = (f32[544,128]{1,0:T(8,128)S(1)}, f32[544,128]{1,0:T(8,128)S(1)}, u32[]{:S(2)}, u32[]{:S(2)}) collective-permute-start(f32[544,128]{1,0:T(8,128)S(1)} %get-tuple-element.35), channel_id=1, source_target_pairs={{0,15},{1,8},{2,9},{3,10},{4,11},{5,12},{6,13},{7,14},{8,23},{9,16... | collective-permute-start | bytes 835592 | tf_op jit(solution)/shard_map/ppermute | solution.py:1036
  47.6 20.4 %own_pairs.1.field_in = f32[257,8,128]{2,1,0:T(8,128)S(1)} custom-call(s32[8,384]{1,0:T(8,128)S(1)} %get-tuple-element.22.words, f32[257,8,128]{2,1,0:T(8,128)S(1)} %bitcast.8, f32[257,8,128]{2,1,0:T(8,128)S(1)} %get-tuple-element.29.field_in), custom_call_target="tpu_custom_call", output_to_operand_aliasing={{}: (2, {})} | custom-call | flops 20000000000 | bytes 2000000 | tf_op jit(solution)/shard_map/own_pairs/pallas_call | solution.py:1081
  68.0 0.0 collective-permute-done.4.in_0
  68.0 0.0 collective-permute-done.5.in_1
  68.0 0.0 collective-permute-done.6.in_2
  68.0 0.0 collective-permute-done.7.in_3
  68.0 0.0 copy-done
  68.1 5.5 %shift_and_evaluate.1 = (f32[4,65536]{1,0:T(4,128)}, f32[257,8,128]{2,1,0:T(8,128)S(1)}) custom-call(s32[256]{0:T(256)S(1)} %copy-done.2, s32[1,256]{1,0:T(1,128)S(1)} %copy-done.3, s32[1,64]{1,0:T(1,128)S(1)} %copy-done.4, f32[2056,128]{1,0:T(8,128)S(1)} %get-tuple-element.21.bodies, ...), custom_call_target="tpu_custom_call", output_to_operand_aliasing={{1}: (4, {})} | custom-call | tf_op jit(solution)/shard_map/shift_and_evaluate/pallas_call | solution.py:1093
  (9 shorter events, 0.0 us)
Async XLA Ops:
  6.2 27.0 %collective-permute-start = (f32[544,128]{1,0:T(8,128)S(1)}, f32[544,128]{1,0:T(8,128)S(1)}, u32[]{:S(2)}, u32[]{:S(2)}) collective-permute-start(f32[544,128]{1,0:T(8,128)S(1)} %get-tuple-element.25), channel_id=1, source_target_pairs={{8,0},{9,1},{10,2},{11,3},{12,4},{13,5},{14,6},{15,7},{16,8},{17,9... | collective-permute-start | bytes 835592 | tf_op jit(solution)/shard_map/ppermute | solution.py:1036
  6.3 26.9 %collective-permute-start.1 = (f32[544,128]{1,0:T(8,128)S(1)}, f32[544,128]{1,0:T(8,128)S(1)}, u32[]{:S(2)}, u32[]{:S(2)}) collective-permute-start(f32[544,128]{1,0:T(8,128)S(1)} %get-tuple-element.26), channel_id=1, source_target_pairs={{1,0},{2,1},{3,2},{4,3},{5,4},{6,5},{7,6},{0,7},{9,8},{10,9},{11,1... | collective-permute-start | bytes 835592 | tf_op jit(solution)/shard_map/ppermute | solution.py:1036
  12.0 21.2 %collective-permute-start.2 = (f32[544,128]{1,0:T(8,128)S(1)}, f32[544,128]{1,0:T(8,128)S(1)}, u32[]{:S(2)}, u32[]{:S(2)}) collective-permute-start(f32[544,128]{1,0:T(8,128)S(1)} %get-tuple-element.27), channel_id=1, source_target_pairs={{9,0},{10,1},{11,2},{12,3},{13,4},{14,5},{15,6},{8,7},{17,8},{18,9... | collective-permute-start | bytes 835592 | tf_op jit(solution)/shard_map/ppermute | solution.py:1036
  13.3 19.8 %collective-permute-start.3 = (f32[544,128]{1,0:T(8,128)S(1)}, f32[544,128]{1,0:T(8,128)S(1)}, u32[]{:S(2)}, u32[]{:S(2)}) collective-permute-start(f32[544,128]{1,0:T(8,128)S(1)} %get-tuple-element.28), channel_id=1, source_target_pairs={{15,0},{8,1},{9,2},{10,3},{11,4},{12,5},{13,6},{14,7},{23,8},{16,9... | collective-permute-start | bytes 835592 | tf_op jit(solution)/shard_map/ppermute | solution.py:1036
  14.7 18.5 %copy-start.1 = (s32[1,3,1024]{2,0,1:T(1,128)S(1)}, s32[1,3,1024]{2,0,1:T(1,128)}, u32[]{:S(2)}) copy-start(s32[1,3,1024]{2,0,1:T(1,128)} %param.16) | copy-start | bytes 36868
  14.7 18.5 %copy-start.5 = (s32[1,3,64]{2,0,1:T(1,128)S(1)}, s32[1,3,64]{2,0,1:T(1,128)}, u32[]{:S(2)}) copy-start(s32[1,3,64]{2,0,1:T(1,128)} %param.17) | copy-start | bytes 2308
  43.9 24.1 %collective-permute-start.4 = (f32[544,128]{1,0:T(8,128)S(1)}, f32[544,128]{1,0:T(8,128)S(1)}, u32[]{:S(2)}, u32[]{:S(2)}) collective-permute-start(f32[544,128]{1,0:T(8,128)S(1)} %get-tuple-element.32), channel_id=1, source_target_pairs={{0,8},{1,9},{2,10},{3,11},{4,12},{5,13},{6,14},{7,15},{8,16},{9,17... | collective-permute-start | bytes 835592 | tf_op jit(solution)/shard_map/ppermute | solution.py:1036
  44.0 24.1 %collective-permute-start.5 = (f32[544,128]{1,0:T(8,128)S(1)}, f32[544,128]{1,0:T(8,128)S(1)}, u32[]{:S(2)}, u32[]{:S(2)}) collective-permute-start(f32[544,128]{1,0:T(8,128)S(1)} %get-tuple-element.33), channel_id=1, source_target_pairs={{0,1},{1,2},{2,3},{3,4},{4,5},{5,6},{6,7},{7,0},{8,9},{9,10},{10,1... | collective-permute-start | bytes 835592 | tf_op jit(solution)/shard_map/ppermute | solution.py:1036
  44.0 24.0 %collective-permute-start.6 = (f32[544,128]{1,0:T(8,128)S(1)}, f32[544,128]{1,0:T(8,128)S(1)}, u32[]{:S(2)}, u32[]{:S(2)}) collective-permute-start(f32[544,128]{1,0:T(8,128)S(1)} %get-tuple-element.34), channel_id=1, source_target_pairs={{0,9},{1,10},{2,11},{3,12},{4,13},{5,14},{6,15},{7,8},{8,17},{9,18... | collective-permute-start | bytes 835592 | tf_op jit(solution)/shard_map/ppermute | solution.py:1036
  44.1 23.9 %collective-permute-start.7 = (f32[544,128]{1,0:T(8,128)S(1)}, f32[544,128]{1,0:T(8,128)S(1)}, u32[]{:S(2)}, u32[]{:S(2)}) collective-permute-start(f32[544,128]{1,0:T(8,128)S(1)} %get-tuple-element.35), channel_id=1, source_target_pairs={{0,15},{1,8},{2,9},{3,10},{4,11},{5,12},{6,13},{7,14},{8,23},{9,16... | collective-permute-start | bytes 835592 | tf_op jit(solution)/shard_map/ppermute | solution.py:1036
  47.6 20.4 %copy-start = (f32[128,1024]{1,0:T(8,128)S(1)}, f32[128,1024]{1,0:T(8,128)}, u32[]{:S(2)}) copy-start(f32[128,1024]{1,0:T(8,128)} %constant.5.clone.down) | copy-start | bytes 1572868
  47.6 20.4 %copy-start.2 = (s32[256]{0:T(256)S(1)}, s32[256]{0:T(256)}, u32[]{:S(2)}) copy-start(s32[256]{0:T(256)} %counts.1) | copy-start | bytes 3076
  47.6 20.4 %copy-start.3 = (s32[1,256]{1,0:T(1,128)S(1)}, s32[1,256]{1,0:T(1,128)}, u32[]{:S(2)}) copy-start(s32[1,256]{1,0:T(1,128)} %send.1) | copy-start | bytes 3076
  47.6 20.4 %copy-start.4 = (s32[1,64]{1,0:T(1,128)S(1)}, s32[1,64]{1,0:T(1,128)}, u32[]{:S(2)}) copy-start(s32[1,64]{1,0:T(1,128)} %send_p.1) | copy-start | bytes 772
where the time goes:
time: 73.2 us; the launch traced here: 73.8 us
  Pallas kernels  61.2 us (84%)
  starting transfers between devices  12.2 us (17%)
    pallas_call x1, Pallas kernels, on_device(): pl.pallas_call(functools.partial(near_kernel, places), out_shape=tiled, i...  20.4 us
    pallas_call x1, Pallas kernels, on_device(): pl.pallas_call(functools.partial(self_kernel, places), out_shape=tiled, i...  18.5 us
    ppermute x8, starting transfers between devices, exchange(): return lax.ppermute(value, ('slab', 'sub'), pairs)  12.2 us
    pallas_call x1, Pallas kernels, on_device(): pl.pallas_call(functools.partial(remote_kernel, places), out_shape=[tiled...  10.7 us
    pallas_call x1, Pallas kernels, on_device(): pl.pallas_call(functools.partial(front_kernel, places), out_shape=[shaped...  6.15 us
    pallas_call x1, Pallas kernels, on_device(): pl.pallas_call(functools.partial(back_kernel, places), out_shape=[shaped(...  5.53 us
  transfers between devices with their start and end apart: 8, of which 0 were waited for; matrix products, arithmetic and copies ran while one was open for 0% of the time, Pallas kernels for 53%

commit v1 on v0

--- a/solution.py
+++ b/solution.py
@@ -83,7 +83,8 @@
                 choose = math.prod(math.comb(a, b) for a, b in zip(alpha, beta))
                 up[at, PLACE[beta], PLACE[alpha]] = choose * power(delta, rest)
                 down[at, PLACE[alpha], PLACE[beta]] = power(delta, rest) / fact(rest)
-    return up.reshape(8 * 128, 128), down.transpose(1, 0, 2).reshape(128, 8 * 128)
+    up = up[:, :FEATS].reshape(8 * FEATS, 128)
+    return up, down[:, :FEATS].transpose(1, 0, 2).reshape(FEATS, 8 * 128)
 
 
 UP, DOWN = shift_matrices()
@@ -445,21 +446,16 @@
         built = jnp.where(lane == CENTRE + 2, cz, built)
         moments[pl.ds(pl.multiple_of(8 * g, 8), 8), :] = built
 
-    batch = 4
-    for u in range(batch):
-        tile(u)
-
-    def group_step(k, carry):
-        groups = [batch * k + u for u in range(batch)]
-        parts = [wide_rows(bodies, g) for g in groups]
-        following = jnp.minimum(batch * (k + 1), LEAVES // 8 - batch)
-        for u in range(batch):
-            tile(following + u)
-        for g, part in zip(groups, parts):
-            cell_moments(g, part)
+    def tile_step(g, carry):
+        tile(g)
         return carry
 
-    lax.fori_loop(0, LEAVES // 8 // batch, group_step, 0)
+    def group_step(g, carry):
+        cell_moments(g, wide_rows(bodies, g))
+        return carry
+
+    lax.fori_loop(0, LEAVES // 8, tile_step, 0, unroll=4)
+    lax.fori_loop(0, LEAVES // 8, group_step, 0, unroll=4)
     kind = row & 3
     bx = place[0].astype(f32) + 0.5
     by = place[1].astype(f32) + 0.5
@@ -475,8 +471,8 @@
             [moments[pl.ds(first + 2 * CZ * py, half_z, stride=2), :] for py in range(CY // 2)], 0
         )
         summed = summed + jnp.dot(
-            piece,
-            up[128 * at : 128 * at + 128, :],
+            piece[:, :FEATS],
+            up[FEATS * at : FEATS * at + FEATS, :],
             precision=lax.Precision.HIGHEST,
             preferred_element_type=f32,
         )
@@ -883,7 +879,7 @@
     half_z = CZ // 2
     for at in range(8):
         moved = jnp.dot(
-            parent_terms[...],
+            parent_terms[:, :FEATS],
             down[:, 128 * at : 128 * at + 128],
             precision=lax.Precision.HIGHEST,
             preferred_element_type=f32,

time: 73.2 us -> 72.5 us (level)
  the two profiles are of different devices: /device:TPU:1 before, /device:TPU:5 now
where the time goes in v1:
time: 72.5 us; the launch traced here: 72.2 us
  Pallas kernels  60 us (83%)
  starting transfers between devices  11.9 us (16%)
    pallas_call x1, Pallas kernels, on_device(): pl.pallas_call(functools.partial(near_kernel, places), out_shape=tiled, i...  20.7 us
    pallas_call x1, Pallas kernels, on_device(): pl.pallas_call(functools.partial(self_kernel, places), out_shape=tiled, i...  18.6 us
    ppermute x8, starting transfers between devices, exchange(): return lax.ppermute(value, ('slab', 'sub'), pairs)  11.9 us
    pallas_call x1, Pallas kernels, on_device(): pl.pallas_call(functools.partial(remote_kernel, places), out_shape=[tiled...  9.88 us
    pallas_call x1, Pallas kernels, on_device(): pl.pallas_call(functools.partial(front_kernel, places), out_shape=[shaped...  5.52 us
    pallas_call x1, Pallas kernels, on_device(): pl.pallas_call(functools.partial(back_kernel, places), out_shape=[shaped(...  5.3 us
  transfers between devices with their start and end apart: 8, of which 0 were waited for; matrix products, arithmetic and copies ran while one was open for 0% of the time, Pallas kernels for 54%

profile of v1, /device:TPU:5, one launch (start us, length us, event | category | flops | bytes accessed | tf_op | source)
XLA Modules:
  0.0 72.2 jit_solution(4972176857169273803)
XLA Ops:
  0.0 5.5 %moments_and_packing.1 = (f32[2056,128]{1,0:T(8,128)S(1)}, f32[256,128]{1,0:T(8,128)S(1)}, f32[32,128]{1,0:T(8,128)S(1)}, s32[8,384]{1,0:T(8,128)S(1)}, f32[544,...) custom-call(s32[1,256]{1,0:T(1,128)} %send.1, s32[1,64]{1,0:T(1,128)} %send_p.1, ...), custom_call_target="tpu_custom_call" | custom-call | tf_op jit(solution)/shard_map/moments_and_packing/pallas_call | solution.py:985
  5.5 0.7 %collective-permute-start = (f32[544,128]{1,0:T(8,128)S(1)}, f32[544,128]{1,0:T(8,128)S(1)}, u32[]{:S(2)}, u32[]{:S(2)}) collective-permute-start(f32[544,128]{1,0:T(8,128)S(1)} %get-tuple-element.25), channel_id=1, source_target_pairs={{8,0},{9,1},{10,2},{11,3},{12,4},{13,5},{14,6},{15,7},{16,8},{17,9... | collective-permute-start | bytes 835592 | tf_op jit(solution)/shard_map/ppermute | solution.py:1032
  6.3 4.2 %collective-permute-start.1 = (f32[544,128]{1,0:T(8,128)S(1)}, f32[544,128]{1,0:T(8,128)S(1)}, u32[]{:S(2)}, u32[]{:S(2)}) collective-permute-start(f32[544,128]{1,0:T(8,128)S(1)} %get-tuple-element.26), channel_id=1, source_target_pairs={{1,0},{2,1},{3,2},{4,3},{5,4},{6,5},{7,6},{0,7},{9,8},{10,9},{11,1... | collective-permute-start | bytes 835592 | tf_op jit(solution)/shard_map/ppermute | solution.py:1032
  10.5 0.5 collective-permute-start.2
  11.0 1.2 %collective-permute-start.3 = (f32[544,128]{1,0:T(8,128)S(1)}, f32[544,128]{1,0:T(8,128)S(1)}, u32[]{:S(2)}, u32[]{:S(2)}) collective-permute-start(f32[544,128]{1,0:T(8,128)S(1)} %get-tuple-element.28), channel_id=1, source_target_pairs={{15,0},{8,1},{9,2},{10,3},{11,4},{12,5},{13,6},{14,7},{23,8},{16,9... | collective-permute-start | bytes 835592 | tf_op jit(solution)/shard_map/ppermute | solution.py:1032
  12.2 18.6 %self_pairs.1.field_in = f32[257,8,128]{2,1,0:T(8,128)S(1)} custom-call(s32[8,384]{1,0:T(8,128)S(1)} %get-tuple-element.22.words, f32[257,8,128]{2,1,0:T(8,128)S(1)} %bitcast.6), custom_call_target="tpu_custom_call" | custom-call | flops 20000000000 | bytes 2000000 | tf_op jit(solution)/shard_map/self_pairs/pallas_call | solution.py:1036
  30.8 0.0 collective-permute-done.in_0
  30.8 0.0 collective-permute-done.1.in_1
  30.9 0.0 collective-permute-done.2.in_2
  30.9 0.0 collective-permute-done.3.in_3
  30.9 0.0 copy-done.1
  30.9 0.0 copy-done.5
  30.9 9.9 %pairs_with_others.1 = (f32[257,8,128]{2,1,0:T(8,128)S(1)}, f32[256,128]{1,0:T(8,128)S(1)}, f32[32,128]{1,0:T(8,128)S(1)}, f32[544,128]{1,0:T(8,128)S(1)}, f32[5...) custom-call(s32[8,384]{1,0:T(8,128)S(1)} %get-tuple-element.22.words, ...), custom_call_target="tpu_custom_call", output_to_operand_aliasing={{0}: (10, {})} | custom-call | tf_op jit(solution)/shard_map/pairs_with_others/pallas_call | solution.py:1049
  40.8 0.1 collective-permute-start.4
  40.9 0.1 collective-permute-start.5
  40.9 0.1 collective-permute-start.6
  41.1 4.9 %collective-permute-start.7 = (f32[544,128]{1,0:T(8,128)S(1)}, f32[544,128]{1,0:T(8,128)S(1)}, u32[]{:S(2)}, u32[]{:S(2)}) collective-permute-start(f32[544,128]{1,0:T(8,128)S(1)} %get-tuple-element.35), channel_id=1, source_target_pairs={{0,15},{1,8},{2,9},{3,10},{4,11},{5,12},{6,13},{7,14},{8,23},{9,16... | collective-permute-start | bytes 835592 | tf_op jit(solution)/shard_map/ppermute | solution.py:1032
  46.0 20.7 %own_pairs.1.field_in = f32[257,8,128]{2,1,0:T(8,128)S(1)} custom-call(s32[8,384]{1,0:T(8,128)S(1)} %get-tuple-element.22.words, f32[257,8,128]{2,1,0:T(8,128)S(1)} %bitcast.8, f32[257,8,128]{2,1,0:T(8,128)S(1)} %get-tuple-element.29.field_in), custom_call_target="tpu_custom_call", output_to_operand_aliasing={{}: (2, {})} | custom-call | flops 20000000000 | bytes 2000000 | tf_op jit(solution)/shard_map/own_pairs/pallas_call | solution.py:1077
  66.7 0.0 collective-permute-done.4.in_0
  66.7 0.0 collective-permute-done.5.in_1
  66.7 0.0 collective-permute-done.6.in_2
  66.7 0.0 collective-permute-done.7.in_3
  66.7 0.0 copy-done
  66.8 5.3 %shift_and_evaluate.1 = (f32[4,65536]{1,0:T(4,128)}, f32[257,8,128]{2,1,0:T(8,128)S(1)}) custom-call(s32[256]{0:T(256)S(1)} %copy-done.2, s32[1,256]{1,0:T(1,128)S(1)} %copy-done.3, s32[1,64]{1,0:T(1,128)S(1)} %copy-done.4, f32[2056,128]{1,0:T(8,128)S(1)} %get-tuple-element.21.bodies, ...), custom_call_target="tpu_custom_call", output_to_operand_aliasing={{1}: (4, {})} | custom-call | tf_op jit(solution)/shard_map/shift_and_evaluate/pallas_call | solution.py:1089
  (9 shorter events, 0.0 us)
Async XLA Ops:
  5.5 25.3 %collective-permute-start = (f32[544,128]{1,0:T(8,128)S(1)}, f32[544,128]{1,0:T(8,128)S(1)}, u32[]{:S(2)}, u32[]{:S(2)}) collective-permute-start(f32[544,128]{1,0:T(8,128)S(1)} %get-tuple-element.25), channel_id=1, source_target_pairs={{8,0},{9,1},{10,2},{11,3},{12,4},{13,5},{14,6},{15,7},{16,8},{17,9... | collective-permute-start | bytes 835592 | tf_op jit(solution)/shard_map/ppermute | solution.py:1032
  6.3 24.6 %collective-permute-start.1 = (f32[544,128]{1,0:T(8,128)S(1)}, f32[544,128]{1,0:T(8,128)S(1)}, u32[]{:S(2)}, u32[]{:S(2)}) collective-permute-start(f32[544,128]{1,0:T(8,128)S(1)} %get-tuple-element.26), channel_id=1, source_target_pairs={{1,0},{2,1},{3,2},{4,3},{5,4},{6,5},{7,6},{0,7},{9,8},{10,9},{11,1... | collective-permute-start | bytes 835592 | tf_op jit(solution)/shard_map/ppermute | solution.py:1032
  10.5 20.4 %collective-permute-start.2 = (f32[544,128]{1,0:T(8,128)S(1)}, f32[544,128]{1,0:T(8,128)S(1)}, u32[]{:S(2)}, u32[]{:S(2)}) collective-permute-start(f32[544,128]{1,0:T(8,128)S(1)} %get-tuple-element.27), channel_id=1, source_target_pairs={{9,0},{10,1},{11,2},{12,3},{13,4},{14,5},{15,6},{8,7},{17,8},{18,9... | collective-permute-start | bytes 835592 | tf_op jit(solution)/shard_map/ppermute | solution.py:1032
  11.0 19.9 %collective-permute-start.3 = (f32[544,128]{1,0:T(8,128)S(1)}, f32[544,128]{1,0:T(8,128)S(1)}, u32[]{:S(2)}, u32[]{:S(2)}) collective-permute-start(f32[544,128]{1,0:T(8,128)S(1)} %get-tuple-element.28), channel_id=1, source_target_pairs={{15,0},{8,1},{9,2},{10,3},{11,4},{12,5},{13,6},{14,7},{23,8},{16,9... | collective-permute-start | bytes 835592 | tf_op jit(solution)/shard_map/ppermute | solution.py:1032
  12.2 18.7 %copy-start.1 = (s32[1,3,1024]{2,0,1:T(1,128)S(1)}, s32[1,3,1024]{2,0,1:T(1,128)}, u32[]{:S(2)}) copy-start(s32[1,3,1024]{2,0,1:T(1,128)} %param.16) | copy-start | bytes 36868
  12.2 18.7 %copy-start.5 = (s32[1,3,64]{2,0,1:T(1,128)S(1)}, s32[1,3,64]{2,0,1:T(1,128)}, u32[]{:S(2)}) copy-start(s32[1,3,64]{2,0,1:T(1,128)} %param.17) | copy-start | bytes 2308
  40.8 25.9 %collective-permute-start.4 = (f32[544,128]{1,0:T(8,128)S(1)}, f32[544,128]{1,0:T(8,128)S(1)}, u32[]{:S(2)}, u32[]{:S(2)}) collective-permute-start(f32[544,128]{1,0:T(8,128)S(1)} %get-tuple-element.32), channel_id=1, source_target_pairs={{0,8},{1,9},{2,10},{3,11},{4,12},{5,13},{6,14},{7,15},{8,16},{9,17... | collective-permute-start | bytes 835592 | tf_op jit(solution)/shard_map/ppermute | solution.py:1032
  40.9 25.8 %collective-permute-start.5 = (f32[544,128]{1,0:T(8,128)S(1)}, f32[544,128]{1,0:T(8,128)S(1)}, u32[]{:S(2)}, u32[]{:S(2)}) collective-permute-start(f32[544,128]{1,0:T(8,128)S(1)} %get-tuple-element.33), channel_id=1, source_target_pairs={{0,1},{1,2},{2,3},{3,4},{4,5},{5,6},{6,7},{7,0},{8,9},{9,10},{10,1... | collective-permute-start | bytes 835592 | tf_op jit(solution)/shard_map/ppermute | solution.py:1032
  40.9 25.8 %collective-permute-start.6 = (f32[544,128]{1,0:T(8,128)S(1)}, f32[544,128]{1,0:T(8,128)S(1)}, u32[]{:S(2)}, u32[]{:S(2)}) collective-permute-start(f32[544,128]{1,0:T(8,128)S(1)} %get-tuple-element.34), channel_id=1, source_target_pairs={{0,9},{1,10},{2,11},{3,12},{4,13},{5,14},{6,15},{7,8},{8,17},{9,18... | collective-permute-start | bytes 835592 | tf_op jit(solution)/shard_map/ppermute | solution.py:1032
  41.1 25.7 %collective-permute-start.7 = (f32[544,128]{1,0:T(8,128)S(1)}, f32[544,128]{1,0:T(8,128)S(1)}, u32[]{:S(2)}, u32[]{:S(2)}) collective-permute-start(f32[544,128]{1,0:T(8,128)S(1)} %get-tuple-element.35), channel_id=1, source_target_pairs={{0,15},{1,8},{2,9},{3,10},{4,11},{5,12},{6,13},{7,14},{8,23},{9,16... | collective-permute-start | bytes 835592 | tf_op jit(solution)/shard_map/ppermute | solution.py:1032
  46.0 20.7 %copy-start = (f32[40,1024]{1,0:T(8,128)S(1)}, f32[40,1024]{1,0:T(8,128)}, u32[]{:S(2)}) copy-start(f32[40,1024]{1,0:T(8,128)} %constant.5.clone.down) | copy-start | bytes 491524
  46.0 20.7 %copy-start.2 = (s32[256]{0:T(256)S(1)}, s32[256]{0:T(256)}, u32[]{:S(2)}) copy-start(s32[256]{0:T(256)} %counts.1) | copy-start | bytes 3076
  46.0 20.7 %copy-start.3 = (s32[1,256]{1,0:T(1,128)S(1)}, s32[1,256]{1,0:T(1,128)}, u32[]{:S(2)}) copy-start(s32[1,256]{1,0:T(1,128)} %send.1) | copy-start | bytes 3076
  46.0 20.7 %copy-start.4 = (s32[1,64]{1,0:T(1,128)S(1)}, s32[1,64]{1,0:T(1,128)}, u32[]{:S(2)}) copy-start(s32[1,64]{1,0:T(1,128)} %send_p.1) | copy-start | bytes 772

commit v2 on v1

--- a/solution.py
+++ b/solution.py
@@ -39,9 +39,8 @@
 TERMS = len(MULTI)
 CENTRE = TERMS
 LIVE = TERMS + 3
-SIZES = (256, 192, 160, 128, 96)
+SIZES = (256, 224, 192, 160, 128, 96)
 EVERY_SIZE = tuple((size, at) for at, size in enumerate(SIZES))
-SOME_SIZES = ((256, 0), (192, 2), (128, 4))
 LIST = 384
 STEPS_AT = LIST - 8
 FEATS = 40
@@ -578,7 +577,7 @@
             if at + 1 < len(SIZES):
                 fits = jnp.logical_and(fits, need > SIZES[at + 1])
             flags.append(jnp.where(jnp.logical_and(member, fits), 1.0, 0.0))
-    flags = jnp.concatenate(flags + [jnp.zeros((16 - len(flags), LEAVES), f32)], 0)
+    flags = jnp.concatenate(flags + [jnp.zeros((32 - len(flags), LEAVES), f32)], 0)
     before = jnp.where(row_ids(wide) < lane_ids(wide), 1.0, 0.0).astype(bf16)
     order = jnp.dot(flags.astype(bf16), before, preferred_element_type=f32)
     number = jnp.sum(flags, axis=1, keepdims=True)
@@ -691,7 +690,7 @@
     far_field[...] = jnp.zeros_like(far_field)
     refs = paired(scratch)
     pair_loop(
-        words, 1, GROUP // 2, SOME_SIZES, place, True, bodies, far_bodies, field, far_field, refs
+        words, 1, GROUP // 2, EVERY_SIZE, place, True, bodies, far_bodies, field, far_field, refs
     )
     for way in range(4):
         outgoing[way][:BODY_ROWS, :] = far_field[way * SLOTS : (way + 1) * SLOTS].reshape(

time: 72.5 us -> 73.8 us (1.018)
  the two profiles are of different devices: /device:TPU:5 before, /device:TPU:1 now
where the time goes in v2:
time: 73.8 us; the launch traced here: 74.7 us
  Pallas kernels  60.3 us (82%)
  starting transfers between devices  14.1 us (19%)
    pallas_call x1, Pallas kernels, on_device(): pl.pallas_call(functools.partial(near_kernel, places), out_shape=tiled, i...  22.7 us
    pallas_call x1, Pallas kernels, on_device(): pl.pallas_call(functools.partial(self_kernel, places), out_shape=tiled, i...  18.1 us
    ppermute x8, starting transfers between devices, exchange(): return lax.ppermute(value, ('slab', 'sub'), pairs)  14.1 us
    pallas_call x1, Pallas kernels, on_device(): pl.pallas_call(functools.partial(remote_kernel, places), out_shape=[tiled...  8.71 us
    pallas_call x1, Pallas kernels, on_device(): pl.pallas_call(functools.partial(front_kernel, places), out_shape=[shaped...  5.53 us
    pallas_call x1, Pallas kernels, on_device(): pl.pallas_call(functools.partial(back_kernel, places), out_shape=[shaped(...  5.3 us
  transfers between devices with their start and end apart: 8, of which 0 were waited for; matrix products, arithmetic and copies ran while one was open for 0% of the time, Pallas kernels for 55%

profile of v2, /device:TPU:1, one launch (start us, length us, event | category | flops | bytes accessed | tf_op | source)
XLA Modules:
  0.0 74.7 jit_solution(8714401052246600861)
XLA Ops:
  0.0 5.5 %moments_and_packing.1 = (f32[2056,128]{1,0:T(8,128)S(1)}, f32[256,128]{1,0:T(8,128)S(1)}, f32[32,128]{1,0:T(8,128)S(1)}, s32[8,384]{1,0:T(8,128)S(1)}, f32[544,...) custom-call(s32[1,256]{1,0:T(1,128)} %send.1, s32[1,64]{1,0:T(1,128)} %send_p.1, ...), custom_call_target="tpu_custom_call" | custom-call | tf_op jit(solution)/shard_map/moments_and_packing/pallas_call | solution.py:984
  5.5 0.1 collective-permute-start
  5.7 5.7 %collective-permute-start.1 = (f32[544,128]{1,0:T(8,128)S(1)}, f32[544,128]{1,0:T(8,128)S(1)}, u32[]{:S(2)}, u32[]{:S(2)}) collective-permute-start(f32[544,128]{1,0:T(8,128)S(1)} %get-tuple-element.26), channel_id=1, source_target_pairs={{1,0},{2,1},{3,2},{4,3},{5,4},{6,5},{7,6},{0,7},{9,8},{10,9},{11,1... | collective-permute-start | bytes 835592 | tf_op jit(solution)/shard_map/ppermute | solution.py:1031
  11.3 1.4 %collective-permute-start.2 = (f32[544,128]{1,0:T(8,128)S(1)}, f32[544,128]{1,0:T(8,128)S(1)}, u32[]{:S(2)}, u32[]{:S(2)}) collective-permute-start(f32[544,128]{1,0:T(8,128)S(1)} %get-tuple-element.27), channel_id=1, source_target_pairs={{9,0},{10,1},{11,2},{12,3},{13,4},{14,5},{15,6},{8,7},{17,8},{18,9... | collective-permute-start | bytes 835592 | tf_op jit(solution)/shard_map/ppermute | solution.py:1031
  12.7 1.3 %collective-permute-start.3 = (f32[544,128]{1,0:T(8,128)S(1)}, f32[544,128]{1,0:T(8,128)S(1)}, u32[]{:S(2)}, u32[]{:S(2)}) collective-permute-start(f32[544,128]{1,0:T(8,128)S(1)} %get-tuple-element.28), channel_id=1, source_target_pairs={{15,0},{8,1},{9,2},{10,3},{11,4},{12,5},{13,6},{14,7},{23,8},{16,9... | collective-permute-start | bytes 835592 | tf_op jit(solution)/shard_map/ppermute | solution.py:1031
  14.1 18.1 %self_pairs.1.field_in = f32[257,8,128]{2,1,0:T(8,128)S(1)} custom-call(s32[8,384]{1,0:T(8,128)S(1)} %get-tuple-element.22.words, f32[257,8,128]{2,1,0:T(8,128)S(1)} %bitcast.6), custom_call_target="tpu_custom_call" | custom-call | flops 20000000000 | bytes 2000000 | tf_op jit(solution)/shard_map/self_pairs/pallas_call | solution.py:1035
  32.1 0.0 collective-permute-done.in_0
  32.2 0.0 collective-permute-done.1.in_1
  32.2 0.0 collective-permute-done.2.in_2
  32.2 0.0 collective-permute-done.3.in_3
  32.2 0.0 copy-done.1
  32.2 0.0 copy-done.5
  32.2 8.7 %pairs_with_others.1 = (f32[257,8,128]{2,1,0:T(8,128)S(1)}, f32[256,128]{1,0:T(8,128)S(1)}, f32[32,128]{1,0:T(8,128)S(1)}, f32[544,128]{1,0:T(8,128)S(1)}, f32[5...) custom-call(s32[8,384]{1,0:T(8,128)S(1)} %get-tuple-element.22.words, ...), custom_call_target="tpu_custom_call", output_to_operand_aliasing={{0}: (10, {})} | custom-call | tf_op jit(solution)/shard_map/pairs_with_others/pallas_call | solution.py:1048
  40.9 1.3 %collective-permute-start.4 = (f32[544,128]{1,0:T(8,128)S(1)}, f32[544,128]{1,0:T(8,128)S(1)}, u32[]{:S(2)}, u32[]{:S(2)}) collective-permute-start(f32[544,128]{1,0:T(8,128)S(1)} %get-tuple-element.32), channel_id=1, source_target_pairs={{0,8},{1,9},{2,10},{3,11},{4,12},{5,13},{6,14},{7,15},{8,16},{9,17... | collective-permute-start | bytes 835592 | tf_op jit(solution)/shard_map/ppermute | solution.py:1031
  42.2 0.0 collective-permute-start.5
  42.2 0.0 collective-permute-start.6
  42.2 4.2 %collective-permute-start.7 = (f32[544,128]{1,0:T(8,128)S(1)}, f32[544,128]{1,0:T(8,128)S(1)}, u32[]{:S(2)}, u32[]{:S(2)}) collective-permute-start(f32[544,128]{1,0:T(8,128)S(1)} %get-tuple-element.35), channel_id=1, source_target_pairs={{0,15},{1,8},{2,9},{3,10},{4,11},{5,12},{6,13},{7,14},{8,23},{9,16... | collective-permute-start | bytes 835592 | tf_op jit(solution)/shard_map/ppermute | solution.py:1031
  46.5 22.7 %own_pairs.1.field_in = f32[257,8,128]{2,1,0:T(8,128)S(1)} custom-call(s32[8,384]{1,0:T(8,128)S(1)} %get-tuple-element.22.words, f32[257,8,128]{2,1,0:T(8,128)S(1)} %bitcast.8, f32[257,8,128]{2,1,0:T(8,128)S(1)} %get-tuple-element.29.field_in), custom_call_target="tpu_custom_call", output_to_operand_aliasing={{}: (2, {})} | custom-call | flops 20000000000 | bytes 2000000 | tf_op jit(solution)/shard_map/own_pairs/pallas_call | solution.py:1076
  69.2 0.0 collective-permute-done.4.in_0
  69.2 0.0 collective-permute-done.5.in_1
  69.2 0.0 collective-permute-done.6.in_2
  69.2 0.0 collective-permute-done.7.in_3
  69.2 0.0 copy-done
  69.2 5.3 %shift_and_evaluate.1 = (f32[4,65536]{1,0:T(4,128)}, f32[257,8,128]{2,1,0:T(8,128)S(1)}) custom-call(s32[256]{0:T(256)S(1)} %copy-done.2, s32[1,256]{1,0:T(1,128)S(1)} %copy-done.3, s32[1,64]{1,0:T(1,128)S(1)} %copy-done.4, f32[2056,128]{1,0:T(8,128)S(1)} %get-tuple-element.21.bodies, ...), custom_call_target="tpu_custom_call", output_to_operand_aliasing={{1}: (4, {})} | custom-call | tf_op jit(solution)/shard_map/shift_and_evaluate/pallas_call | solution.py:1088
  (9 shorter events, 0.0 us)
Async XLA Ops:
  5.5 26.6 %collective-permute-start = (f32[544,128]{1,0:T(8,128)S(1)}, f32[544,128]{1,0:T(8,128)S(1)}, u32[]{:S(2)}, u32[]{:S(2)}) collective-permute-start(f32[544,128]{1,0:T(8,128)S(1)} %get-tuple-element.25), channel_id=1, source_target_pairs={{8,0},{9,1},{10,2},{11,3},{12,4},{13,5},{14,6},{15,7},{16,8},{17,9... | collective-permute-start | bytes 835592 | tf_op jit(solution)/shard_map/ppermute | solution.py:1031
  5.7 26.5 %collective-permute-start.1 = (f32[544,128]{1,0:T(8,128)S(1)}, f32[544,128]{1,0:T(8,128)S(1)}, u32[]{:S(2)}, u32[]{:S(2)}) collective-permute-start(f32[544,128]{1,0:T(8,128)S(1)} %get-tuple-element.26), channel_id=1, source_target_pairs={{1,0},{2,1},{3,2},{4,3},{5,4},{6,5},{7,6},{0,7},{9,8},{10,9},{11,1... | collective-permute-start | bytes 835592 | tf_op jit(solution)/shard_map/ppermute | solution.py:1031
  11.3 20.8 %collective-permute-start.2 = (f32[544,128]{1,0:T(8,128)S(1)}, f32[544,128]{1,0:T(8,128)S(1)}, u32[]{:S(2)}, u32[]{:S(2)}) collective-permute-start(f32[544,128]{1,0:T(8,128)S(1)} %get-tuple-element.27), channel_id=1, source_target_pairs={{9,0},{10,1},{11,2},{12,3},{13,4},{14,5},{15,6},{8,7},{17,8},{18,9... | collective-permute-start | bytes 835592 | tf_op jit(solution)/shard_map/ppermute | solution.py:1031
  12.7 19.5 %collective-permute-start.3 = (f32[544,128]{1,0:T(8,128)S(1)}, f32[544,128]{1,0:T(8,128)S(1)}, u32[]{:S(2)}, u32[]{:S(2)}) collective-permute-start(f32[544,128]{1,0:T(8,128)S(1)} %get-tuple-element.28), channel_id=1, source_target_pairs={{15,0},{8,1},{9,2},{10,3},{11,4},{12,5},{13,6},{14,7},{23,8},{16,9... | collective-permute-start | bytes 835592 | tf_op jit(solution)/shard_map/ppermute | solution.py:1031
  14.1 18.1 %copy-start.1 = (s32[1,3,1024]{2,0,1:T(1,128)S(1)}, s32[1,3,1024]{2,0,1:T(1,128)}, u32[]{:S(2)}) copy-start(s32[1,3,1024]{2,0,1:T(1,128)} %param.16) | copy-start | bytes 36868
  14.1 18.1 %copy-start.5 = (s32[1,3,64]{2,0,1:T(1,128)S(1)}, s32[1,3,64]{2,0,1:T(1,128)}, u32[]{:S(2)}) copy-start(s32[1,3,64]{2,0,1:T(1,128)} %param.17) | copy-start | bytes 2308
  40.9 28.2 %collective-permute-start.4 = (f32[544,128]{1,0:T(8,128)S(1)}, f32[544,128]{1,0:T(8,128)S(1)}, u32[]{:S(2)}, u32[]{:S(2)}) collective-permute-start(f32[544,128]{1,0:T(8,128)S(1)} %get-tuple-element.32), channel_id=1, source_target_pairs={{0,8},{1,9},{2,10},{3,11},{4,12},{5,13},{6,14},{7,15},{8,16},{9,17... | collective-permute-start | bytes 835592 | tf_op jit(solution)/shard_map/ppermute | solution.py:1031
  42.2 26.9 %collective-permute-start.5 = (f32[544,128]{1,0:T(8,128)S(1)}, f32[544,128]{1,0:T(8,128)S(1)}, u32[]{:S(2)}, u32[]{:S(2)}) collective-permute-start(f32[544,128]{1,0:T(8,128)S(1)} %get-tuple-element.33), channel_id=1, source_target_pairs={{0,1},{1,2},{2,3},{3,4},{4,5},{5,6},{6,7},{7,0},{8,9},{9,10},{10,1... | collective-permute-start | bytes 835592 | tf_op jit(solution)/shard_map/ppermute | solution.py:1031
  42.2 26.9 %collective-permute-start.6 = (f32[544,128]{1,0:T(8,128)S(1)}, f32[544,128]{1,0:T(8,128)S(1)}, u32[]{:S(2)}, u32[]{:S(2)}) collective-permute-start(f32[544,128]{1,0:T(8,128)S(1)} %get-tuple-element.34), channel_id=1, source_target_pairs={{0,9},{1,10},{2,11},{3,12},{4,13},{5,14},{6,15},{7,8},{8,17},{9,18... | collective-permute-start | bytes 835592 | tf_op jit(solution)/shard_map/ppermute | solution.py:1031
  42.2 26.9 %collective-permute-start.7 = (f32[544,128]{1,0:T(8,128)S(1)}, f32[544,128]{1,0:T(8,128)S(1)}, u32[]{:S(2)}, u32[]{:S(2)}) collective-permute-start(f32[544,128]{1,0:T(8,128)S(1)} %get-tuple-element.35), channel_id=1, source_target_pairs={{0,15},{1,8},{2,9},{3,10},{4,11},{5,12},{6,13},{7,14},{8,23},{9,16... | collective-permute-start | bytes 835592 | tf_op jit(solution)/shard_map/ppermute | solution.py:1031
  46.5 22.7 %copy-start = (f32[40,1024]{1,0:T(8,128)S(1)}, f32[40,1024]{1,0:T(8,128)}, u32[]{:S(2)}) copy-start(f32[40,1024]{1,0:T(8,128)} %constant.5.clone.down) | copy-start | bytes 491524
  46.5 22.7 %copy-start.2 = (s32[256]{0:T(256)S(1)}, s32[256]{0:T(256)}, u32[]{:S(2)}) copy-start(s32[256]{0:T(256)} %counts.1) | copy-start | bytes 3076
  46.5 22.7 %copy-start.3 = (s32[1,256]{1,0:T(1,128)S(1)}, s32[1,256]{1,0:T(1,128)}, u32[]{:S(2)}) copy-start(s32[1,256]{1,0:T(1,128)} %send.1) | copy-start | bytes 3076
  46.5 22.7 %copy-start.4 = (s32[1,64]{1,0:T(1,128)S(1)}, s32[1,64]{1,0:T(1,128)}, u32[]{:S(2)}) copy-start(s32[1,64]{1,0:T(1,128)} %send_p.1) | copy-start | bytes 772
